TPU v7x, 32 devices: a whole 2x2x4 slice. The times are simulated.
32 devices in a mesh: chan: 8 (over z, y), tm: 4 (over x, core).
Axes of the slice: x: 2, y: 2, z: 4, core: 2. Of those that a mesh axis runs over, the one named last changes fastest.
Arguments:
- recording: bfloat16 [4096, 8192], P('chan', 'tm'), may hold values from -6 to 6
- band_taps: bfloat16 [3, 255], replicated, may hold values from -0.375 to 0.375
- channel_gain: float32 [4096], P('chan'), may hold values from 0.25 to 2
- range_test: bfloat16 [8192, 64], P('tm'), may hold values from -0.0625 to 0.0625
- corange_test: bfloat16 [64, 4096], P(None, 'chan'), may hold values from -0.09375 to 0.09375
- core_left: bfloat16 [128, 4096], P(None, 'chan'), may hold values from -0.09375 to 0.09375
- core_right: bfloat16 [8192, 128], P('tm'), may hold values from -0.0625 to 0.0625
Outputs:
- strain_rate: bfloat16 [3, 4096, 8192], P(None, 'chan', 'tm')
- range_sketch: float32 [3, 4096, 64], P(None, 'chan')
- corange_sketch: float32 [3, 64, 8192], P(None, None, 'tm')
- core_sketch: float32 [3, 128, 128], replicated
All inputs are finite; a program needn't handle non-finite values.
Results may differ from a plain program's by a relative error of at most 0.0052.
Values may be sent and summed in bfloat16 or wider, within the bound.
A program may use at most 64 MiB of HBM per device.

v0:
```python
import jax
import jax.numpy as jnp
from jax import lax
from jax.sharding import PartitionSpec as P


def padded_2(block, sides, width):
    for axis, dim in sides:
        count = lax.axis_size(axis)
        forward = [(i, i + 1) for i in range(count - 1)]
        backward = [(target, source) for source, target in forward]
        low = lax.ppermute(
            lax.slice_in_dim(block, block.shape[dim] - width, None, axis=dim), axis, forward
        )
        high = lax.ppermute(lax.slice_in_dim(block, 0, width, axis=dim), axis, backward)
        block = jnp.concatenate([low, block, high], axis=dim)
    return block


def on_device(recording, band_taps, channel_gain, range_test, corange_test, core_left, core_right):
    tap_count = band_taps.shape[1]
    half_width = tap_count // 2
    channels, samples = recording.shape
    padded = padded_2(recording, (("tm", 1),), half_width)
    padded = jnp.pad(padded, ((0, 0), (0, 256 - 2 * half_width)))
    blocks = samples // 128
    lead_block = padded[:, :samples].reshape(channels, blocks, 128)
    mid_block = padded[:, 128 : samples + 128].reshape(channels, blocks, 128)
    tail_block = padded[:, 256 : samples + 256].reshape(channels, blocks, 128)
    windows = jnp.concatenate([lead_block, mid_block, tail_block], axis=2)
    window_pos = lax.broadcasted_iota(jnp.int32, (384, 128), 0)
    output_pos = lax.broadcasted_iota(jnp.int32, (384, 128), 1)
    offset = window_pos - output_pos
    inside = (offset >= 0) & (offset < tap_count)
    picked = jnp.take(band_taps, jnp.clip(offset, 0, tap_count - 1), axis=1)
    toeplitz = jnp.where(inside[None], picked, jnp.zeros_like(picked))
    band_count = band_taps.shape[0]
    filtered = jnp.einsum("cnw,bwo->bcno", windows, toeplitz, preferred_element_type=jnp.float32)
    filtered = filtered.reshape(band_count, channels, samples).astype(jnp.bfloat16)
    rimmed = padded_2(filtered, (("chan", 1),), 1)
    difference = rimmed[:, 2:].astype(jnp.float32) - rimmed[:, :-2].astype(jnp.float32)
    strain_rate = (channel_gain[None, :, None] * difference).astype(jnp.bfloat16)
    range_part = jnp.einsum(
        "bct,tk->bck", strain_rate, range_test, preferred_element_type=jnp.float32
    )
    corange_part = jnp.einsum(
        "lc,bct->blt", corange_test, strain_rate, preferred_element_type=jnp.float32
    )
    high = lax.Precision.HIGHEST
    projected = jnp.einsum(
        "bct,ts->bcs", strain_rate, core_right, preferred_element_type=jnp.float32
    )
    range_sketch, projected_sum = lax.psum((range_part, projected), "tm")
    corange_sketch = lax.psum(corange_part, "chan")
    core_term = jnp.einsum(
        "rc,bcs->brs", core_left.astype(jnp.float32), projected_sum, precision=high
    )
    core_sketch = lax.psum(core_term, "chan")
    return (strain_rate, range_sketch, corange_sketch, core_sketch)


def solution(mesh):
    in_specs = (
        P("chan", "tm"),
        P(),
        P("chan"),
        P("tm", None),
        P(None, "chan"),
        P(None, "chan"),
        P("tm", None),
    )
    out_specs = (P(None, "chan", "tm"), P(None, "chan", None), P(None, None, "tm"), P())
    return jax.shard_map(
        on_device, mesh=mesh, in_specs=in_specs, out_specs=out_specs, check_vma=False
    )
```

profile of v0, /device:TPU:0, one launch (start us, length us, event | category | flops | bytes accessed | tf_op | source)
XLA Modules:
  0.0 424.9 jit_solution(13206108507670665187)
XLA Ops:
  7.2 0.0 copy-start
  7.2 0.0 all-reduce.8.cloned.1.call-start
  7.2 2.9 copy.20
  10.1 0.7 fusion.31
  10.9 2.4 collective-permute-start
  13.2 1.3 collective-permute-start.1
  14.5 0.1 fusion.16
  14.6 0.8 copy.18
  15.4 170.7 %gather_fusion = bf16[49152,3]{1,0:T(8,128)(2,1)} fusion(bf16[3,255]{0,1:T(8,128)(2,1)S(1)} %copy.18, s32[49152]{0:T(1024)S(1)} %fusion.16), kind=kCustom, calls=%fused_computation | custom fusion | bytes 786432 | tf_op jit(solution)/shard_map/jit(_take)/gather | solution.py:35
  186.2 16.1 %copy.19 = bf16[384,128,3]{0,1,2:T(8,128)(2,1)S(1)} copy(bf16[384,128,3]{2,1,0:T(8,128)(2,1)} %bitcast.43) | data formatting | bytes 589824 | tf_op jit(solution)/shard_map/jit(_take)/gather | solution.py:35
  202.3 0.1 fusion.21
  202.4 0.0 collective-permute-done
  202.4 0.0 collective-permute-done.1
  202.4 11.3 %concatenate.21 = bf16[512,2302]{0,1:T(8,128)(2,1)} concatenate(bf16[512,127]{0,1:T(8,128)(2,1)S(1)} %collective-permute-done, bf16[512,2048]{0,1:T(8,128)(2,1)S(1)} %copy.20, bf16[512,127]{0,1:T(8,128)(2,1)S(1)} %collective-permute-done.1), dimensions={1} | concatenate | bytes 4714496 | tf_op jit(solution)/shard_map/concatenate | solution.py:16
  213.7 3.1 pad_slice_fusion
  216.8 3.9 copy.27
  220.7 2.5 pad_maximum_fusion.3
  223.2 4.1 copy.26
  227.3 3.9 copy.25
  231.2 0.0 copy-done.2
  231.2 6.9 %fusion.5 = bf16[3,128,512,16]{2,1,3,0:T(8,128)(2,1)} fusion(bf16[512,16,128]{2,0,1:T(8,128)(2,1)S(1)} %copy-done.2, bf16[512,16,128]{2,0,1:T(8,128)(2,1)} %copy.26, bf16[512,16,128]{2,0,1:T(8,128)(2,1)} %copy.25, bf16[384,128,3]{0,1,2:T(8,128)(2,1)S(1)} %copy.19, pred[384,128]{0,1:T(8,128)(4,1)S(1)} %get-tuple-element.23, ...), kind=kOutput, calls=%fused_computation.10 | convolution fusion | flops 2438234112 | bytes 12976128 | tf_op jit(solution)/shard_map/cnw,bwo->bcno/dot_general | solution.py:38
  238.1 8.9 %copy.29 = bf16[3,512,2048]{2,1,0:T(8,128)(2,1)} copy(bf16[3,512,2048]{1,2,0:T(8,128)(2,1)} %bitcast.47) | data formatting | bytes 12582912 | tf_op jit(solution)/shard_map/convert_element_type | solution.py:39
  247.0 1.0 fusion.30
  248.0 4.3 %collective-permute-start.3 = (bf16[3,1,2048]{2,1,0:T(2,128)(2,1)S(1)}, bf16[3,1,2048]{2,1,0:T(2,128)(2,1)S(1)}, u32[]{:S(2)}, u32[]{:S(2)}) collective-permute-start(bf16[3,1,2048]{2,1,0:T(2,128)(2,1)S(1)} %get-tuple-element.17), channel_id=1, source_target_pairs={{0,4},{4,8},{8,12},{12,16},{16,20},{20,24},{24,28},{1,5},{5,9},{9,... | collective-permute-start | bytes 36872 | tf_op jit(solution)/shard_map/ppermute | solution.py:12
  252.3 0.0 copy-start.3
  252.3 1.4 collective-permute-start.2
  253.7 0.1 collective-permute-done.3
  253.8 4.4 %collective-permute-done.2 = bf16[3,1,2048]{2,1,0:T(2,128)(2,1)S(1)} collective-permute-done((bf16[3,1,2048]{2,1,0:T(2,128)(2,1)S(1)}, bf16[3,1,2048]{2,1,0:T(2,128)(2,1)S(1)}, u32[]{:S(2)}, u32[]{:S(2)}) %collective-permute-start.2) | collective-permute-done | bytes 12320 | tf_op jit(solution)/shard_map/ppermute | solution.py:15
  258.2 0.0 copy-done.6
  258.2 8.3 %multiply_convert_fusion = bf16[3,512,2048]{2,1,0:T(8,128)(2,1)S(1)} fusion(bf16[3,512,2048]{2,1,0:T(8,128)(2,1)} %copy.29, bf16[3,1,2048]{2,1,0:T(2,128)(2,1)S(1)} %collective-permute-done.3, bf16[3,1,2048]{2,1,0:T(2,128)(2,1)S(1)} %collective-permute-done.2, f32[512]{0:T(512)S(1)} %copy-done.6), kind=kLoop, calls=%fused_computation.1 | loop fusion | flops 34603008 | bytes 12609536 | tf_op jit(solution)/shard_map/convert_element_type | solution.py:42
  266.4 0.0 copy-done.3
  266.4 0.0 copy-start.1
  266.4 0.0 copy-start.5
  266.5 2.8 fusion.13
  269.3 0.0 copy-done.1
  269.3 0.0 copy-done
  269.3 3.1 fusion.6
  272.4 0.0 all-reduce.8.cloned.1.call-update
  272.4 0.0 all-reduce.6.cloned.1.call-start
  272.5 0.0 copy-done.5
  272.5 5.1 %convolution_bitcast_fusion = f32[3,64,2048]{2,1,0:T(8,128)} fusion(bf16[3,512,2048]{2,1,0:T(8,128)(2,1)} %copy-done.1, bf16[64,512]{1,0:T(8,128)(2,1)S(1)} %copy-done.5), kind=kOutput, calls=%fused_computation.11 | convolution fusion | flops 402653184 | bytes 7929856 | tf_op jit(solution)/shard_map/lc,bct->blt/dot_general | solution.py:46
  277.6 36.1 %all-reduce.8.cloned.1.call-done = (f32[3,512,64]{1,2,0:T(8,128)}, f32[3,512,128]{1,2,0:T(8,128)}) async-done(((f32[3,512,64]{1,2,0:T(8,128)}, f32[3,512,128]{1,2,0:T(8,128)}), (f32[3,512,64]{1,2,0:T(8,128)}, f32[3,512,128]{1,2,0:T(8,128)})) %all-reduce.8.cloned.1.call-update) | async-done | bytes 1179664 | tf_op jit(solution)/shard_map/psum | solution.py:53
  313.7 2.3 convolution_bitcast_fusion.1
  316.0 0.0 all-reduce.6.cloned.1.call-update
  316.0 95.8 %all-reduce.6.cloned.1.call-done = (f32[3,64,2048]{2,1,0:T(8,128)}, f32[3,128,128]{1,2,0:T(8,128)}) async-done(((f32[3,64,2048]{2,1,0:T(8,128)}, f32[3,128,128]{1,2,0:T(8,128)}), (f32[3,64,2048]{2,1,0:T(8,128)}, f32[3,128,128]{1,2,0:T(8,128)})) %all-reduce.6.cloned.1.call-update) | async-done | bytes 1769488 | tf_op jit(solution)/shard_map/psum | solution.py:54
  411.8 1.7 copy.32
  413.6 1.8 copy.38
  415.3 2.7 copy.39
  (4 shorter events, 0.0 us)
Async XLA Ops:
  7.2 262.1 %copy-start = (bf16[2048,128]{1,0:T(8,128)(2,1)S(1)}, bf16[2048,128]{1,0:T(8,128)(2,1)}, u32[]{:S(2)}) copy-start(bf16[2048,128]{1,0:T(8,128)(2,1)} %param.13) | copy-start | bytes 1572868
  7.2 306.5 %all-reduce.8.cloned.1.call-start = ((), (), s32[]{:S(2)}) async-start(), calls=%async_computation.1 | async-start | bytes 2359296 | tf_op jit(solution)/shard_map/psum | solution.py:53
  10.9 191.5 %collective-permute-start = (bf16[512,127]{0,1:T(8,128)(2,1)}, bf16[512,127]{0,1:T(8,128)(2,1)S(1)}, u32[]{:S(2)}, u32[]{:S(2)}) collective-permute-start(bf16[512,127]{0,1:T(8,128)(2,1)} %get-tuple-element.21), channel_id=1, source_target_pairs={{0,1},{1,2},{2,3},{4,5},{5,6},{6,7},{8,9},{9,10},{10,11},{12,13},{... | collective-permute-start | bytes 390152 | tf_op jit(solution)/shard_map/ppermute | solution.py:12
  13.2 189.1 %collective-permute-start.1 = (bf16[512,127]{0,1:T(8,128)(2,1)}, bf16[512,127]{0,1:T(8,128)(2,1)S(1)}, u32[]{:S(2)}, u32[]{:S(2)}) collective-permute-start(bf16[512,127]{0,1:T(8,128)(2,1)} %get-tuple-element.20), channel_id=1, source_target_pairs={{1,0},{2,1},{3,2},{5,4},{6,5},{7,6},{9,8},{10,9},{11,10},{13,12},{... | collective-permute-start | bytes 390152 | tf_op jit(solution)/shard_map/ppermute | solution.py:15
  223.2 8.0 %copy-start.2 = (bf16[512,16,128]{2,0,1:T(8,128)(2,1)S(1)}, bf16[512,16,128]{2,0,1:T(8,128)(2,1)}, u32[]{:S(2)}) copy-start(bf16[512,16,128]{2,0,1:T(8,128)(2,1)} %copy.27) | copy-start | bytes 6291460
  238.1 20.1 %copy-start.6 = (f32[512]{0:T(512)S(1)}, f32[512]{0:T(512)}, u32[]{:S(2)}) copy-start(f32[512]{0:T(512)} %param.9) | copy-start | bytes 6148
  248.0 5.8 %collective-permute-start.3 = (bf16[3,1,2048]{2,1,0:T(2,128)(2,1)S(1)}, bf16[3,1,2048]{2,1,0:T(2,128)(2,1)S(1)}, u32[]{:S(2)}, u32[]{:S(2)}) collective-permute-start(bf16[3,1,2048]{2,1,0:T(2,128)(2,1)S(1)} %get-tuple-element.17), channel_id=1, source_target_pairs={{0,4},{4,8},{8,12},{12,16},{16,20},{20,24},{24,28},{1,5},{5,9},{9,... | collective-permute-start | bytes 36872 | tf_op jit(solution)/shard_map/ppermute | solution.py:12
  252.3 14.1 %copy-start.3 = (bf16[2048,64]{0,1:T(8,128)(2,1)S(1)}, bf16[2048,64]{0,1:T(8,128)(2,1)}, u32[]{:S(2)}) copy-start(bf16[2048,64]{0,1:T(8,128)(2,1)} %param.10) | copy-start | bytes 786436
  252.3 5.9 %collective-permute-start.2 = (bf16[3,1,2048]{2,1,0:T(2,128)(2,1)S(1)}, bf16[3,1,2048]{2,1,0:T(2,128)(2,1)S(1)}, u32[]{:S(2)}, u32[]{:S(2)}) collective-permute-start(bf16[3,1,2048]{2,1,0:T(2,128)(2,1)S(1)} %get-tuple-element.16), channel_id=1, source_target_pairs={{4,0},{8,4},{12,8},{16,12},{20,16},{24,20},{28,24},{5,1},{9,5},{13... | collective-permute-start | bytes 36872 | tf_op jit(solution)/shard_map/ppermute | solution.py:15
  266.4 2.8 copy-start.1
  266.4 6.0 %copy-start.5 = (bf16[64,512]{1,0:T(8,128)(2,1)S(1)}, bf16[64,512]{1,0:T(8,128)(2,1)}, u32[]{:S(2)}) copy-start(bf16[64,512]{1,0:T(8,128)(2,1)} %param.11) | copy-start | bytes 196612
  272.4 41.3 %copy-start.4 = (bf16[128,512]{1,0:T(8,128)(2,1)S(1)}, bf16[128,512]{1,0:T(8,128)(2,1)}, u32[]{:S(2)}) copy-start(bf16[128,512]{1,0:T(8,128)(2,1)} %param.12) | copy-start | bytes 393220
  272.4 139.4 %all-reduce.6.cloned.1.call-start = ((), (), s32[]{:S(2)}) async-start(), calls=%async_computation | async-start | bytes 3538944 | tf_op jit(solution)/shard_map/psum | solution.py:54
Sparse Core Ops, SparseCore 0:
  272.5 41.1 all-reduce.7
  317.9 93.9 all-reduce.5
where the time goes:
time: 427 us; the launch traced here: 425 us
  local copies, waits for them, and re-layouts  234 us (55%)
  waiting for transfers between devices  136 us (32%)
  matrix products  20.3 us (5%)
  between operations  14.2 us (3%)
  other arithmetic  10.9 us (3%)
  starting transfers between devices  9.4 us (2%)
    gather x2, local copies, waits for them, and re-layouts, on_device(): picked = jnp.take(band_taps, jnp.clip(offset, 0, tap_count - 1), axis=1)  187 us
    psum x1, waiting for transfers between devices, on_device(): corange_sketch = lax.psum(corange_part, 'chan')  95.8 us
    psum x1, waiting for transfers between devices, on_device(): range_sketch, projected_sum = lax.psum((range_part, projected), 'tm')  36.1 us
    concatenate x1, local copies, waits for them, and re-layouts, padded_2(): block = jnp.concatenate([low, block, high], axis=dim)  11.3 us
    unnamed x19, local copies, waits for them, and re-layouts  9.98 us
    convert_element_type x1, local copies, waits for them, and re-layouts, on_device(): filtered.reshape(band_count, channels, samples).astype(jnp.bfloat16)  8.93 us
  transfers between devices with their start and end apart: 6, of which 4 were waited for; matrix products, arithmetic and copies ran while one was open for 45% of the time, Pallas kernels for 0%

commit v1 on v0

--- a/solution.py
+++ b/solution.py
@@ -51,7 +51,10 @@
         "bct,ts->bcs", strain_rate, core_right, preferred_element_type=jnp.float32
     )
     range_sketch, projected_sum = lax.psum((range_part, projected), "tm")
-    corange_sketch = lax.psum(corange_part, "chan")
+    size, corange_sketch = (lax.axis_size("chan"), corange_part)
+    for far in [1 << k for k in range(size.bit_length() - 1)]:
+        swap = [(i_2, i_2 ^ far) for i_2 in range(size)]
+        corange_sketch = corange_sketch + lax.ppermute(corange_sketch, "chan", swap)
     core_term = jnp.einsum(
         "rc,bcs->brs", core_left.astype(jnp.float32), projected_sum, precision=high
     )

time: 427 us -> 483 us (1.13)
  waiting for transfers between devices: 136 us -> 190 us
  starting transfers between devices: 9.4 us -> 16.2 us
    ppermute x0 -> x3, waiting for transfers between devices: none -> 69.8 us  [on_device(): corange_sketch = corange_sketch + lax.ppermute(corange_sketch, 'chan', swap)]
    psum x1, waiting for transfers between devices: 95.8 us -> 79.5 us  [on_device(): core_sketch = lax.psum(core_term, 'chan')]
    ppermute x0 -> x3, starting transfers between devices: none -> 6.78 us  [on_device(): corange_sketch = corange_sketch + lax.ppermute(corange_sketch, 'chan', swap)]
    unnamed x19 -> x20, local copies, waits for them, and re-layouts: 9.98 us -> 6.26 us
  transfers between devices with their start and end apart: 6 -> 9, of which waited for: 4 -> 6; matrix products, arithmetic and copies ran while one was open for 45% -> 41% of each run, Pallas kernels for 0% -> 0%
where the time goes in v1:
time: 483 us; the launch traced here: 481 us
  local copies, waits for them, and re-layouts  230 us (48%)
  waiting for transfers between devices  190 us (39%)
  matrix products  16.4 us (3%)
  starting transfers between devices  16.2 us (3%)
  between operations  14.2 us (3%)
  other arithmetic  14.1 us (3%)
    gather x2, local copies, waits for them, and re-layouts, on_device(): picked = jnp.take(band_taps, jnp.clip(offset, 0, tap_count - 1), axis=1)  187 us
    psum x1, waiting for transfers between devices, on_device(): core_sketch = lax.psum(core_term, 'chan')  79.5 us
    ppermute x3, waiting for transfers between devices, on_device(): corange_sketch = corange_sketch + lax.ppermute(corange_sketch, 'chan', swap)  69.8 us
    psum x1, waiting for transfers between devices, on_device(): range_sketch, projected_sum = lax.psum((range_part, projected), 'tm')  36.4 us
    concatenate x1, local copies, waits for them, and re-layouts, padded_2(): block = jnp.concatenate([low, block, high], axis=dim)  11.3 us
  transfers between devices with their start and end apart: 9, of which 6 were waited for; matrix products, arithmetic and copies ran while one was open for 41% of the time, Pallas kernels for 0%

profile of v1, /device:TPU:0, one launch (start us, length us, event | category | flops | bytes accessed | tf_op | source)
XLA Modules:
  0.0 481.0 jit_solution(14583345309252918488)
XLA Ops:
  7.2 0.0 copy-start
  7.2 0.0 all-reduce.7.cloned.1.call-start
  7.2 2.9 copy.20
  10.1 0.7 fusion.31
  10.9 2.4 collective-permute-start
  13.2 1.3 collective-permute-start.1
  14.5 0.1 fusion.16
  14.6 0.8 copy.18
  15.4 170.7 %gather_fusion = bf16[49152,3]{1,0:T(8,128)(2,1)} fusion(bf16[3,255]{0,1:T(8,128)(2,1)S(1)} %copy.18, s32[49152]{0:T(1024)S(1)} %fusion.16), kind=kCustom, calls=%fused_computation | custom fusion | bytes 786432 | tf_op jit(solution)/shard_map/jit(_take)/gather | solution.py:35
  186.1 16.1 %copy.19 = bf16[384,128,3]{0,1,2:T(8,128)(2,1)S(1)} copy(bf16[384,128,3]{2,1,0:T(8,128)(2,1)} %bitcast.43) | data formatting | bytes 589824 | tf_op jit(solution)/shard_map/jit(_take)/gather | solution.py:35
  202.2 0.1 fusion.21
  202.3 11.3 %concatenate.21 = bf16[512,2302]{0,1:T(8,128)(2,1)} concatenate(bf16[512,127]{0,1:T(8,128)(2,1)S(1)} %collective-permute-done, bf16[512,2048]{0,1:T(8,128)(2,1)S(1)} %copy.20, bf16[512,127]{0,1:T(8,128)(2,1)S(1)} %collective-permute-done.1), dimensions={1} | concatenate | bytes 4714496 | tf_op jit(solution)/shard_map/concatenate | solution.py:16
  213.6 3.1 pad_slice_fusion
  216.7 3.9 copy.27
  220.6 2.5 pad_maximum_fusion.3
  223.1 4.0 copy.26
  227.2 3.9 copy.25
  231.1 6.9 %fusion.5 = bf16[3,128,512,16]{2,1,3,0:T(8,128)(2,1)} fusion(bf16[512,16,128]{2,0,1:T(8,128)(2,1)S(1)} %copy-done.2, bf16[512,16,128]{2,0,1:T(8,128)(2,1)} %copy.26, bf16[512,16,128]{2,0,1:T(8,128)(2,1)} %copy.25, bf16[384,128,3]{0,1,2:T(8,128)(2,1)S(1)} %copy.19, pred[384,128]{0,1:T(8,128)(4,1)S(1)} %get-tuple-element.21, ...), kind=kOutput, calls=%fused_computation.10 | convolution fusion | flops 2438234112 | bytes 12976128 | tf_op jit(solution)/shard_map/cnw,bwo->bcno/dot_general | solution.py:38
  238.0 8.9 %copy.29 = bf16[3,512,2048]{2,1,0:T(8,128)(2,1)} copy(bf16[3,512,2048]{1,2,0:T(8,128)(2,1)} %bitcast.47) | data formatting | bytes 12582912 | tf_op jit(solution)/shard_map/convert_element_type | solution.py:39
  246.9 1.0 fusion.30
  247.9 4.3 collective-permute-start.3
  252.2 0.0 copy-start.6
  252.2 1.4 collective-permute-start.2
  253.6 0.1 collective-permute-done.3
  253.7 4.4 collective-permute-done.2
  258.1 8.3 %multiply_convert_fusion = bf16[3,512,2048]{2,1,0:T(8,128)(2,1)S(1)} fusion(bf16[3,512,2048]{2,1,0:T(8,128)(2,1)} %copy.29, bf16[3,1,2048]{2,1,0:T(2,128)(2,1)S(1)} %collective-permute-done.3, bf16[3,1,2048]{2,1,0:T(2,128)(2,1)S(1)} %collective-permute-done.2, f32[512]{0:T(512)S(1)} %copy-done.7), kind=kLoop, calls=%fused_computation.1 | loop fusion | flops 34603008 | bytes 12609536 | tf_op jit(solution)/shard_map/convert_element_type | solution.py:42
  266.3 0.0 copy-start.1
  266.3 1.3 convolution_bitcast_fusion
  267.6 0.0 copy-start.4
  267.6 2.5 collective-permute-start.4
  270.1 35.0 %collective-permute-done.4 = f32[3,64,2048]{2,1,0:T(8,128)S(1)} collective-permute-done((f32[3,64,2048]{2,1,0:T(8,128)S(1)}, f32[3,64,2048]{2,1,0:T(8,128)S(1)}, u32[]{:S(2)}, u32[]{:S(2)}) %collective-permute-start.4) | collective-permute-done | bytes 1572896 | tf_op jit(solution)/shard_map/ppermute | solution.py:57
  305.1 0.2 add.36
  305.3 1.6 collective-permute-start.5
  306.9 34.8 %collective-permute-done.5 = f32[3,64,2048]{2,1,0:T(8,128)S(1)} collective-permute-done((f32[3,64,2048]{2,1,0:T(8,128)S(1)}, f32[3,64,2048]{2,1,0:T(8,128)S(1)}, u32[]{:S(2)}, u32[]{:S(2)}) %collective-permute-start.5) | collective-permute-done | bytes 1572896 | tf_op jit(solution)/shard_map/ppermute | solution.py:57
  341.8 0.2 add.37
  342.0 0.0 copy-start.5
  342.0 2.7 collective-permute-start.6
  344.7 2.8 fusion.13
  347.4 3.1 fusion.6
  350.5 0.0 all-reduce.7.cloned.1.call-update
  350.6 0.0 all-reduce.5.cloned.1.call-start
  350.6 36.4 %all-reduce.7.cloned.1.call-done = (f32[3,512,64]{1,2,0:T(8,128)}, f32[3,512,128]{1,2,0:T(8,128)}) async-done(((f32[3,512,64]{1,2,0:T(8,128)}, f32[3,512,128]{1,2,0:T(8,128)}), (f32[3,512,64]{1,2,0:T(8,128)}, f32[3,512,128]{1,2,0:T(8,128)})) %all-reduce.7.cloned.1.call-update) | async-done | bytes 1179664 | tf_op jit(solution)/shard_map/psum | solution.py:53
  387.0 2.4 convolution_bitcast_fusion.1
  389.4 0.0 all-reduce.5.cloned.1.call-update
  389.4 79.5 %all-reduce.5.cloned.1.call-done = f32[3,128,128]{1,2,0:T(8,128)} async-done(((f32[3,128,128]{1,2,0:T(8,128)}), f32[3,128,128]{1,2,0:T(8,128)}) %all-reduce.5.cloned.1.call-update) | async-done | bytes 196624 | tf_op jit(solution)/shard_map/psum | solution.py:61
  468.9 1.7 copy.32
  470.6 2.7 add.38
  473.4 0.7 copy.37
  (14 shorter events, 0.0 us)
Async XLA Ops:
  7.2 340.3 %copy-start = (bf16[2048,128]{1,0:T(8,128)(2,1)S(1)}, bf16[2048,128]{1,0:T(8,128)(2,1)}, u32[]{:S(2)}) copy-start(bf16[2048,128]{1,0:T(8,128)(2,1)} %param.13) | copy-start | bytes 1572868
  7.2 379.9 %all-reduce.7.cloned.1.call-start = ((), (), s32[]{:S(2)}) async-start(), calls=%async_computation.1 | async-start | bytes 2359296 | tf_op jit(solution)/shard_map/psum | solution.py:53
  10.9 191.4 %collective-permute-start = (bf16[512,127]{0,1:T(8,128)(2,1)}, bf16[512,127]{0,1:T(8,128)(2,1)S(1)}, u32[]{:S(2)}, u32[]{:S(2)}) collective-permute-start(bf16[512,127]{0,1:T(8,128)(2,1)} %get-tuple-element.19), channel_id=1, source_target_pairs={{0,1},{1,2},{2,3},{4,5},{5,6},{6,7},{8,9},{9,10},{10,11},{12,13},{... | collective-permute-start | bytes 390152 | tf_op jit(solution)/shard_map/ppermute | solution.py:12
  13.2 189.1 %collective-permute-start.1 = (bf16[512,127]{0,1:T(8,128)(2,1)}, bf16[512,127]{0,1:T(8,128)(2,1)S(1)}, u32[]{:S(2)}, u32[]{:S(2)}) collective-permute-start(bf16[512,127]{0,1:T(8,128)(2,1)} %get-tuple-element.18), channel_id=1, source_target_pairs={{1,0},{2,1},{3,2},{5,4},{6,5},{7,6},{9,8},{10,9},{11,10},{13,12},{... | collective-permute-start | bytes 390152 | tf_op jit(solution)/shard_map/ppermute | solution.py:15
  223.1 8.0 %copy-start.2 = (bf16[512,16,128]{2,0,1:T(8,128)(2,1)S(1)}, bf16[512,16,128]{2,0,1:T(8,128)(2,1)}, u32[]{:S(2)}) copy-start(bf16[512,16,128]{2,0,1:T(8,128)(2,1)} %copy.27) | copy-start | bytes 6291460
  238.0 20.0 %copy-start.7 = (f32[512]{0:T(512)S(1)}, f32[512]{0:T(512)}, u32[]{:S(2)}) copy-start(f32[512]{0:T(512)} %param.9) | copy-start | bytes 6148
  247.9 5.8 %collective-permute-start.3 = (bf16[3,1,2048]{2,1,0:T(2,128)(2,1)S(1)}, bf16[3,1,2048]{2,1,0:T(2,128)(2,1)S(1)}, u32[]{:S(2)}, u32[]{:S(2)}) collective-permute-start(bf16[3,1,2048]{2,1,0:T(2,128)(2,1)S(1)} %get-tuple-element.15), channel_id=1, source_target_pairs={{0,4},{4,8},{8,12},{12,16},{16,20},{20,24},{24,28},{1,5},{5,9},{9,... | collective-permute-start | bytes 36872 | tf_op jit(solution)/shard_map/ppermute | solution.py:12
  252.2 14.1 %copy-start.6 = (bf16[64,512]{1,0:T(8,128)(2,1)S(1)}, bf16[64,512]{1,0:T(8,128)(2,1)}, u32[]{:S(2)}) copy-start(bf16[64,512]{1,0:T(8,128)(2,1)} %param.11) | copy-start | bytes 196612
  252.2 5.9 %collective-permute-start.2 = (bf16[3,1,2048]{2,1,0:T(2,128)(2,1)S(1)}, bf16[3,1,2048]{2,1,0:T(2,128)(2,1)S(1)}, u32[]{:S(2)}, u32[]{:S(2)}) collective-permute-start(bf16[3,1,2048]{2,1,0:T(2,128)(2,1)S(1)} %get-tuple-element.14), channel_id=1, source_target_pairs={{4,0},{8,4},{12,8},{16,12},{20,16},{24,20},{28,24},{5,1},{9,5},{13... | collective-permute-start | bytes 36872 | tf_op jit(solution)/shard_map/ppermute | solution.py:15
  266.3 81.1 %copy-start.1 = (bf16[3,512,2048]{2,1,0:T(8,128)(2,1)}, bf16[3,512,2048]{2,1,0:T(8,128)(2,1)S(1)}, u32[]{:S(2)}) copy-start(bf16[3,512,2048]{2,1,0:T(8,128)(2,1)S(1)} %multiply_convert_fusion) | copy-start | bytes 18874372
  267.6 77.1 %copy-start.4 = (bf16[2048,64]{0,1:T(8,128)(2,1)S(1)}, bf16[2048,64]{0,1:T(8,128)(2,1)}, u32[]{:S(2)}) copy-start(bf16[2048,64]{0,1:T(8,128)(2,1)} %param.10) | copy-start | bytes 786436
  267.6 37.5 %collective-permute-start.4 = (f32[3,64,2048]{2,1,0:T(8,128)S(1)}, f32[3,64,2048]{2,1,0:T(8,128)S(1)}, u32[]{:S(2)}, u32[]{:S(2)}) collective-permute-start(f32[3,64,2048]{2,1,0:T(8,128)S(1)} %convolution_bitcast_fusion), channel_id=1, source_target_pairs={{0,4},{4,0},{8,12},{12,8},{16,20},{20,16},{24,28},{28,24},{1,5},{5... | collective-permute-start | bytes 4718600 | tf_op jit(solution)/shard_map/ppermute | solution.py:57
  305.3 36.5 %collective-permute-start.5 = (f32[3,64,2048]{2,1,0:T(8,128)S(1)}, f32[3,64,2048]{2,1,0:T(8,128)S(1)}, u32[]{:S(2)}, u32[]{:S(2)}) collective-permute-start(f32[3,64,2048]{2,1,0:T(8,128)S(1)} %add.36), channel_id=1, source_target_pairs={{0,8},{4,12},{8,0},{12,4},{16,24},{20,28},{24,16},{28,20},{1,9},{5... | collective-permute-start | bytes 4718600 | tf_op jit(solution)/shard_map/ppermute | solution.py:57
  342.0 45.0 %copy-start.5 = (bf16[128,512]{1,0:T(8,128)(2,1)S(1)}, bf16[128,512]{1,0:T(8,128)(2,1)}, u32[]{:S(2)}) copy-start(bf16[128,512]{1,0:T(8,128)(2,1)} %param.12) | copy-start | bytes 393220
  342.0 128.6 %collective-permute-start.6 = (f32[3,64,2048]{2,1,0:T(8,128)S(1)}, f32[3,64,2048]{2,1,0:T(8,128)}, u32[]{:S(2)}, u32[]{:S(2)}) collective-permute-start(f32[3,64,2048]{2,1,0:T(8,128)S(1)} %add.37), channel_id=1, source_target_pairs={{0,16},{4,20},{8,24},{12,28},{16,0},{20,4},{24,8},{28,12},{1,17},{... | collective-permute-start | bytes 4718600 | tf_op jit(solution)/shard_map/ppermute | solution.py:57
  350.6 118.3 %all-reduce.5.cloned.1.call-start = ((), (), s32[]{:S(2)}) async-start(), calls=%async_computation | async-start | bytes 393216 | tf_op jit(solution)/shard_map/psum | solution.py:61
  387.0 86.3 %copy-start.3 = (f32[3,512,64]{1,2,0:T(8,128)S(1)}, f32[3,512,64]{1,2,0:T(8,128)}, u32[]{:S(2)}) copy-start(f32[3,512,64]{1,2,0:T(8,128)} %get-tuple-element.23) | copy-start | bytes 1179652
Sparse Core Ops, SparseCore 0:
  350.7 36.2 all-reduce.6
  390.9 77.9 all-reduce.4
